TPU v7x, 32 devices: a whole 2x2x4 slice. The times are simulated.
32 devices in a mesh: dp: 8 (over y, x, core), sp: 4 (over z).
Axes of the slice: x: 2, y: 2, z: 4, core: 2. Of those that a mesh axis runs over, the one named last changes fastest.
Arguments:
- tokens: bfloat16 [8, 4096, 768], P('dp', 'sp'), may hold values from -6 to 6
- qkv_weight: bfloat16 [768, 2304], P(('dp', 'sp')), may hold values from -0.21875 to 0.21875
- query_value_bias: bfloat16 [2, 768], P(None, ('dp', 'sp')), may hold values from -3 to 3
- out_weight: bfloat16 [768, 768], P(('dp', 'sp')), may hold values from -1.75 to 1.75
- out_bias: bfloat16 [768], P(('dp', 'sp')), may hold values from -3 to 3
- norm1_gain: bfloat16 [768], P(('dp', 'sp')), may hold values from 0.099609375 to 1.8984375
- norm1_bias: bfloat16 [768], P(('dp', 'sp')), may hold values from -3 to 3
- up_weight: bfloat16 [768, 3072], P(('dp', 'sp')), may hold values from -0.21875 to 0.21875
- up_bias: bfloat16 [3072], P(('dp', 'sp')), may hold values from -3 to 3
- down_weight: bfloat16 [3072, 768], P(('dp', 'sp')), may hold values from -0.109375 to 0.109375
- down_bias: bfloat16 [768], P(('dp', 'sp')), may hold values from -3 to 3
- norm2_gain: bfloat16 [768], P(('dp', 'sp')), may hold values from 0.099609375 to 1.8984375
- norm2_bias: bfloat16 [768], P(('dp', 'sp')), may hold values from -3 to 3
- rand_blocks: int32 [8, 12, 62, 3], P('dp', 'sp'), may hold values from 1 to 62, as said below
- out_grad: bfloat16 [8, 4096, 768], P('dp', 'sp'), may hold values from -6 to 6
Outputs:
- layer_out: bfloat16 [8, 4096, 768], P('dp', 'sp')
- input_grad: float32 [8, 4096, 768], P('dp', 'sp')
- qkv_weight_grad: float32 [768, 2304], P(('dp', 'sp'))
- query_value_bias_grad: float32 [2, 768], P(None, ('dp', 'sp'))
- out_weight_grad: float32 [768, 768], P(('dp', 'sp'))
- out_bias_grad: float32 [768], P(('dp', 'sp'))
- norm1_gain_grad: float32 [768], P(('dp', 'sp'))
- norm1_bias_grad: float32 [768], P(('dp', 'sp'))
- up_weight_grad: float32 [768, 3072], P(('dp', 'sp'))
- up_bias_grad: float32 [3072], P(('dp', 'sp'))
- down_weight_grad: float32 [3072, 768], P(('dp', 'sp'))
- down_bias_grad: float32 [768], P(('dp', 'sp'))
- norm2_gain_grad: float32 [768], P(('dp', 'sp'))
- norm2_bias_grad: float32 [768], P(('dp', 'sp'))
Inputs may be any that keep to these rules, and one draw needn't show every extreme that they name: For middle query block i, the 3 entries of rand_blocks[b, h, i - 1] are distinct and none of them is i - 1, i, i + 1, 0 or 63.
All inputs are finite; a program needn't handle non-finite values.
Results may differ from a plain program's by a relative error of at most 0.013.
Values may be sent and summed in bfloat16 or wider, within the bound.
A program may use at most 256 MiB of HBM per device.

v0:
```python
from functools import partial

import jax
import jax.numpy as jnp
import numpy as np
from jax import lax
from jax.experimental import pallas as pl
from jax.experimental.pallas import tpu as pltpu
from jax.sharding import Mesh
from jax.sharding import PartitionSpec as P

HEAD_DIM = 64
BLOCK = 64
LANES = 128
SLOT = 4 * HEAD_DIM
EPS = 1e-05
MASKED = -1e30
ALL = ("c", "core", "zh", "zl")
GROUP = ("core", "zl")
REST = ("c", "zh")
CHUNK = 512
ROWS = 256
PAIR = 2
SUBS = 1
PAIR_BACK = 2
VMEM_BYTES = 60 * 1024 * 1024

f32 = jnp.float32
bf16 = jnp.bfloat16
NT = (((1,), (1,)), ((), ()))
TN = (((0,), (0,)), ((), ()))


def dot(a, b):
    return jnp.dot(a, b, preferred_element_type=f32)


def dot_nt(a, b):
    return lax.dot_general(a, b, NT, preferred_element_type=f32)


def dot_tn(a, b):
    return lax.dot_general(a, b, TN, preferred_element_type=f32)


def rows_at(start, size):
    return pl.ds(pl.multiple_of(start, size), size)


def listed(ref, rand_ref, head, i, blocks, randoms):
    cols = slice(head * SLOT + LANES, head * SLOT + SLOT)
    near = jnp.clip(i - 1, 0, blocks - 3)
    parts = [ref[0, :, cols], ref[blocks - 1, :, cols]]
    parts += [ref[near + n, :, cols] for n in range(3)]
    base = (head * (blocks - 2) + near) * randoms
    parts += [ref[rand_ref[base + r], :, cols] for r in range(randoms)]
    return jnp.concatenate(parts, axis=0)


def keys_values(ref, head, t, size):
    cols = slice(head * SLOT + LANES, head * SLOT + SLOT)
    return ref[pl.ds(t * (size // BLOCK), size // BLOCK), :, cols].reshape(size, LANES)


def mask_globals(s, i, blocks):
    lane = lax.broadcasted_iota(jnp.int32, (BLOCK, LANES), 1)
    low = lane < BLOCK
    dead = (low & (i == 1)) | (~low & (i == blocks - 2))
    return jnp.concatenate([jnp.where(dead, MASKED, s[:, :LANES]), s[:, LANES:]], axis=1)


def middle_blocks(qkv_ref, rand_ref, res_ref, first, heads, randoms, blocks):
    lane = lax.broadcasted_iota(jnp.int32, (BLOCK, LANES), 1)
    work = [(first + n, h) for n in range(PAIR) for h in range(heads)]
    kvs = [listed(qkv_ref, rand_ref, h, i, blocks, randoms) for i, h in work]
    qs = [qkv_ref[i, :, h * SLOT : h * SLOT + LANES] for i, h in work]
    ss = [mask_globals(dot_nt(q, kv), i, blocks) for q, kv, (i, h) in zip(qs, kvs, work)]
    tops = [jnp.max(s, axis=1, keepdims=True) for s in ss]
    es = [jnp.exp(s - top) for s, top in zip(ss, tops)]
    totals = [jnp.sum(e, axis=1, keepdims=True) for e in es]
    os = [dot(e.astype(bf16), kv) for e, kv in zip(es, kvs)]
    for o, top, total, (i, h) in zip(os, tops, totals, work):
        both = jnp.where(lane < HEAD_DIM, top + jnp.log(total), o / total)
        res_ref[h, rows_at(i * BLOCK, BLOCK), :] = both


def global_blocks(qkv_ref, heads, length):
    last = length // BLOCK - 1

    def ends(h):
        cols = slice(h * SLOT, h * SLOT + LANES)
        return jnp.concatenate([qkv_ref[0, :, cols], qkv_ref[last, :, cols]], axis=0)

    qs = [ends(h) for h in range(heads)]

    def whole(t, carry):
        kvs = [keys_values(qkv_ref, h, t, CHUNK) for h in range(heads)]
        ss = [dot_nt(q, kv) for q, kv in zip(qs, kvs)]
        news = [jnp.maximum(c[0], jnp.max(s, axis=1, keepdims=True)) for c, s in zip(carry, ss)]
        fades = [jnp.exp(c[0] - new) for c, new in zip(carry, news)]
        es = [jnp.exp(s - new) for s, new in zip(ss, news)]
        sums = [jnp.sum(e, axis=1, keepdims=True) for e in es]
        os = [dot(e.astype(bf16), kv) for e, kv in zip(es, kvs)]
        return tuple(
            (new, c[1] * fade + total, c[2] * fade + o)
            for c, new, fade, total, o in zip(carry, news, fades, sums, os)
        )

    start = (
        jnp.full((2 * BLOCK, 1), MASKED, f32),
        jnp.zeros((2 * BLOCK, 1), f32),
        jnp.zeros((2 * BLOCK, LANES), f32),
    )
    done = lax.fori_loop(0, length // CHUNK, whole, (start,) * heads)
    lane = lax.broadcasted_iota(jnp.int32, (2 * BLOCK, LANES), 1)
    return [jnp.where(lane < HEAD_DIM, top + jnp.log(total), acc / total) for top, total, acc in done]


def pack_rows(res_ref, ctx_ref, start, part, piece):
    low = lax.broadcasted_iota(jnp.int32, (BLOCK, LANES), 1) < HEAD_DIM
    for n in range(ROWS // BLOCK):
        rows = rows_at(start + n * BLOCK, BLOCK)
        first = pltpu.roll(res_ref[0, rows, :], HEAD_DIM, 1)
        pair = jnp.where(low, first, res_ref[1, rows, :])
        ctx_ref[part, piece, n * BLOCK : (n + 1) * BLOCK, :] = pair.astype(bf16)
    for n in range(ROWS // (2 * BLOCK)):
        rows = rows_at(start + 2 * n * BLOCK, BLOCK)
        odd = rows_at(start + (2 * n + 1) * BLOCK, BLOCK)
        first = pltpu.roll(res_ref[2, rows, :], HEAD_DIM, 1)
        both = jnp.where(low, first, res_ref[2, odd, :])
        ctx_ref[part, piece, ROWS + n * BLOCK : ROWS + (n + 1) * BLOCK, :] = both.astype(bf16)


def attend_kernel(heads, randoms, rand_ref, x_ref, w_ref, b_ref, qkv_ref, res_ref, ctx_ref):
    length = x_ref.shape[0]
    blocks = length // BLOCK

    def project(t, carry):
        raw = dot(x_ref[rows_at(t * CHUNK, CHUNK), :], w_ref[...]) + b_ref[...]
        step = CHUNK // BLOCK
        qkv_ref[pl.ds(t * step, step)] = raw.astype(bf16).reshape(step, BLOCK, raw.shape[1])
        return carry

    lax.fori_loop(0, length // CHUNK, project, 0)

    def middle(t, carry):
        middle_blocks(qkv_ref, rand_ref, res_ref, t * PAIR, heads, randoms, blocks)
        return carry

    lax.fori_loop(0, blocks // PAIR, middle, 0)
    for h, both in enumerate(global_blocks(qkv_ref, heads, length)):
        res_ref[h, 0:BLOCK, :] = both[:BLOCK]
        res_ref[h, length - BLOCK : length, :] = both[BLOCK:]
    per_quarter = ctx_ref.shape[1]

    def pack(t, carry):
        pack_rows(res_ref, ctx_ref, t * ROWS, t // per_quarter, t % per_quarter)
        return carry

    lax.fori_loop(0, length // ROWS, pack, 0)


def attend(rand, x, w, b, parts, heads):
    length = x.shape[0]
    randoms = rand.size // (heads * (length // BLOCK - 2))
    vmem = pl.BlockSpec(memory_space=pltpu.VMEM)
    return pl.pallas_call(
        partial(attend_kernel, heads, randoms),
        out_shape=(
            jax.ShapeDtypeStruct((length // BLOCK, BLOCK, heads * SLOT), bf16),
            jax.ShapeDtypeStruct((heads, length, LANES), f32),
            jax.ShapeDtypeStruct((parts, length // parts // ROWS, ROWS * 3 // 2, LANES), bf16),
        ),
        in_specs=[pl.BlockSpec(memory_space=pltpu.SMEM), vmem, vmem, vmem],
        out_specs=(vmem, vmem, vmem),
        compiler_params=pltpu.CompilerParams(vmem_limit_bytes=VMEM_BYTES),
        name="attend",
    )(rand, x, w, b)


def attend_back_kernel(
    heads, randoms, rand_ref, qkv_ref, res_ref, dctx_ref, draw_ref, sums_ref, *scratch
):
    dout, acc = scratch[:heads], scratch[heads:]
    blocks = qkv_ref.shape[0]
    length = blocks * BLOCK
    last = (blocks - 1) * BLOCK
    per_quarter = dctx_ref.shape[1]

    def unpack(t, carry):
        part, piece = t // per_quarter, t % per_quarter
        lane = lax.broadcasted_iota(jnp.int32, (BLOCK, LANES), 1)
        low = lane < HEAD_DIM
        for n in range(ROWS // BLOCK):
            rows = rows_at(t * ROWS + n * BLOCK, BLOCK)
            pair = dctx_ref[part, piece, n * BLOCK : (n + 1) * BLOCK, :].astype(f32)
            dout[0][rows, :] = jnp.where(low, 0.0, pltpu.roll(pair, HEAD_DIM, 1)).astype(bf16)
            dout[1][rows, :] = jnp.where(low, 0.0, pair).astype(bf16)
        for n in range(ROWS // (2 * BLOCK)):
            rows = rows_at(t * ROWS + 2 * n * BLOCK, BLOCK)
            odd = rows_at(t * ROWS + (2 * n + 1) * BLOCK, BLOCK)
            both = dctx_ref[part, piece, ROWS + n * BLOCK : ROWS + (n + 1) * BLOCK, :].astype(f32)
            dout[2][rows, :] = jnp.where(low, 0.0, pltpu.roll(both, HEAD_DIM, 1)).astype(bf16)
            dout[2][odd, :] = jnp.where(low, 0.0, both).astype(bf16)
        return carry

    lax.fori_loop(0, length // ROWS, unpack, 0)

    step = 256

    def ends(ref, cols):
        return jnp.concatenate([ref[0:BLOCK, cols], ref[last : last + BLOCK, cols]], axis=0)

    every = slice(0, LANES)
    gs = [ends(dout[h], every) for h in range(heads)]
    reses = [ends(res_ref.at[h], every) for h in range(heads)]
    alls = [
        jnp.concatenate(
            [qkv_ref[n, :, h * SLOT : h * SLOT + LANES] for n in (0, blocks - 1)] + [gs[h]], axis=0
        )
        for h in range(heads)
    ]
    logs = [res[:, 0:1] for res in reses]
    deltas = [jnp.sum(g.astype(f32) * res, axis=1, keepdims=True) for g, res in zip(gs, reses)]

    def whole(t, dqs):
        rows = rows_at(t * step, step)
        kvs = [keys_values(qkv_ref, h, t, step) for h in range(heads)]
        sds = [dot_nt(both, kv) for both, kv in zip(alls, kvs)]
        ps = [jnp.exp(sd[: 2 * BLOCK] - log) for sd, log in zip(sds, logs)]
        dss = [(p * (sd[2 * BLOCK :] - d)).astype(bf16) for p, sd, d in zip(ps, sds, deltas)]
        dkvs = [
            dot_tn(jnp.concatenate([ds, p.astype(bf16)], axis=0), both)
            for ds, p, both in zip(dss, ps, alls)
        ]
        news = tuple(dq + dot(ds, kv) for dq, ds, kv in zip(dqs, dss, kvs))
        for h in range(heads):
            acc[h][rows, :] = dkvs[h]
        return news

    dqs = lax.fori_loop(
        0, length // step, whole, (jnp.zeros((2 * BLOCK, LANES), f32),) * heads
    )
    for h in range(heads):
        cols = slice(h * SLOT, h * SLOT + LANES)
        lane = lax.broadcasted_iota(jnp.int32, (2 * BLOCK, LANES), 1)
        dq = jnp.where(lane < HEAD_DIM, dqs[h], 0.0).astype(bf16)
        draw_ref[0:BLOCK, cols] = dq[:BLOCK]
        draw_ref[last : last + BLOCK, cols] = dq[BLOCK:]

    def middle(t, carry):
        lane = lax.broadcasted_iota(jnp.int32, (BLOCK, LANES), 1)
        work = [(1 + t * PAIR_BACK + n, h) for n in range(PAIR_BACK) for h in range(heads)]
        kvs = [listed(qkv_ref, rand_ref, h, i, blocks, randoms) for i, h in work]
        places = [(rows_at(i * BLOCK, BLOCK), slice(h * SLOT, h * SLOT + LANES)) for i, h in work]
        gs = [dout[h][rows, :] for (rows, _), (_, h) in zip(places, work)]
        reses = [res_ref[h, rows, :] for (rows, _), (_, h) in zip(places, work)]
        alls = [
            jnp.concatenate([qkv_ref[i, :, cols], g], axis=0)
            for (_, cols), (i, _), g in zip(places, work, gs)
        ]
        sds = [dot_nt(both, kv) for both, kv in zip(alls, kvs)]
        deltas = [jnp.sum(g.astype(f32) * res, axis=1, keepdims=True) for g, res in zip(gs, reses)]
        ps = [
            jnp.exp(mask_globals(sd[:BLOCK], i, blocks) - res[:, 0:1])
            for sd, res, (i, h) in zip(sds, reses, work)
        ]
        dss = [(p * (sd[BLOCK:] - d)).astype(bf16) for p, sd, d in zip(ps, sds, deltas)]
        dkvs = [
            dot_tn(jnp.concatenate([ds, p.astype(bf16)], axis=0), both)
            for ds, p, both in zip(dss, ps, alls)
        ]
        dqs = [dot(ds, kv) for ds, kv in zip(dss, kvs)]
        for dq, (rows, cols) in zip(dqs, places):
            draw_ref[rows, cols] = jnp.where(lane < HEAD_DIM, dq, 0.0).astype(bf16)
        for dkv, (i, h) in zip(dkvs, work):
            acc[h][0:BLOCK, :] += dkv[0:BLOCK]
            acc[h][last : last + BLOCK, :] += dkv[BLOCK : 2 * BLOCK]
            near = pl.ds(pl.multiple_of((i - 1) * BLOCK, BLOCK), 3 * BLOCK)
            acc[h][near, :] += dkv[2 * BLOCK : 5 * BLOCK]
            base = (h * (blocks - 2) + i - 1) * randoms
            for r in range(randoms):
                far = rows_at(rand_ref[base + r] * BLOCK, BLOCK)
                acc[h][far, :] += dkv[(5 + r) * BLOCK : (6 + r) * BLOCK]
        return carry

    lax.fori_loop(0, (blocks - 2) // PAIR_BACK, middle, 0)
    sums_ref[...] = jnp.zeros_like(sums_ref)

    def finish(t, carry):
        rows = rows_at(t * CHUNK, CHUNK)
        for h in range(heads):
            at = h * SLOT
            draw_ref[rows, at + LANES : at + SLOT] = acc[h][rows, :].astype(bf16)
        sums_ref[0:1, :] += jnp.sum(draw_ref[rows, :].astype(f32), axis=0, keepdims=True)
        return carry

    lax.fori_loop(0, length // CHUNK, finish, 0)


def attend_back(rand, qkv, res, dctx, heads):
    length = qkv.shape[0] * BLOCK
    randoms = rand.size // (heads * (length // BLOCK - 2))
    vmem = pl.BlockSpec(memory_space=pltpu.VMEM)
    return pl.pallas_call(
        partial(attend_back_kernel, heads, randoms),
        out_shape=(
            jax.ShapeDtypeStruct((length, heads * SLOT), bf16),
            jax.ShapeDtypeStruct((8, heads * SLOT), f32),
        ),
        in_specs=[pl.BlockSpec(memory_space=pltpu.SMEM), vmem, vmem, vmem],
        out_specs=(vmem, vmem),
        scratch_shapes=[pltpu.VMEM((length, LANES), bf16)] * heads
        + [pltpu.VMEM((length, LANES), f32)] * heads,
        compiler_params=pltpu.CompilerParams(vmem_limit_bytes=VMEM_BYTES),
        name="attend_back",
    )(rand, qkv, res, dctx)


def mean_of(a):
    return jnp.mean(a, axis=1, keepdims=True)


def norm(r):
    center = r - mean_of(r)
    rstd = lax.rsqrt(mean_of(center * center) + EPS)
    return center * rstd, rstd


def norm_back(dn, n, rstd):
    return rstd * (dn - mean_of(dn) - n * mean_of(dn * n))


def rowsum(a):
    return jnp.sum(a, axis=0, keepdims=True)


MESH = pl.DeviceIdType.MESH


def run_phases(items):
    step = 0
    live = list(items)
    while live:
        after = []
        for first, phases in live:
            if first > step or next(phases, None) is not None:
                after.append((first, phases))
        live = after
        step += 1


class Where:
    def __init__(self):
        c, core, zh, zl = (lax.axis_index(a) for a in ALL)
        self.y, self.x, self.core, self.zh, self.zl = c // 2, c % 2, core, zh, zl
        self.z = zh * 2 + zl
        self.by_x = (self.y * 2 + 1 - self.x, core, zh, zl)
        self.by_y = ((1 - self.y) * 2 + self.x, core, zh, zl)
        self.by_core = (c, 1 - core, zh, zl)
        self.by_zl = (c, core, zh, 1 - zl)
        self.by_zh = (c, core, 1 - zh, zl)
        self.by_mid = (c, core, 1 - zh, 1 - zl)
        self.by_swap = (c, 1 - core, 1 - zh, zl)
        self.by_both = (c, 1 - core, zh, 1 - zl)
        self.inner = zh != zl
        self.stays = core == zh

    def greet(self):
        barrier = pltpu.get_barrier_semaphore()
        others = (self.by_x, self.by_y, self.by_core, self.by_zl)
        others += (self.by_zh, self.by_mid, self.by_swap, self.by_both)
        for other in others:
            pl.semaphore_signal(barrier, inc=1, device_id=other, device_id_type=MESH)
        pl.semaphore_wait(barrier, len(others))


class Copies:
    def __init__(self, send, recv, local):
        self.send, self.recv, self.local_sems = send, recv, local
        self.n = self.m = 0

    def remote(self, src, dst, device):
        n = self.n
        self.n += 1
        return pltpu.make_async_remote_copy(
            src_ref=src,
            dst_ref=dst,
            send_sem=self.send.at[n],
            recv_sem=self.recv.at[n],
            device_id=device,
            device_id_type=MESH,
        )

    def local(self, src, dst):
        m = self.m
        self.m += 1
        return pltpu.make_async_copy(src, dst, self.local_sems.at[m])


def chain_kernel(
    groups,
    direct,
    ctx_ref,
    tok_ref,
    og_ref,
    wo_ref,
    wu_ref,
    wd_ref,
    vec_ref,
    bu_ref,
    out_ref,
    dres_ref,
    dctx_ref,
    mix_ref,
    hid_ref,
    act_ref,
    dpre_ref,
    dffn_ref,
    dproj_ref,
    gvec_ref,
    gbu_ref,
    slope_ref,
    wop_ref,
    *stage,
):
    width = tok_ref.shape[1]
    hidden = wu_ref.shape[1]
    wide = 3 * HEAD_DIM
    step = pl.program_id(0)
    if direct:
        me = Where()
        out_far, dctx_far = out_ref, dctx_ref
        out_stage, dctx_stage, send, recv, local = stage
        out_ref, dctx_ref = out_stage.at[step], dctx_stage.at[step]

        @pl.when(step == 0)
        def _():
            me.greet()

    def transfers(t):
        place = me.core * 2 + me.zl
        near, beside = me.core * 2 + 1 - me.zl, (1 - me.core) * 2 + me.zl
        across = (1 - me.core) * 2 + 1 - me.zl
        others = ((near, me.by_zl), (beside, me.by_core), (across, me.by_both))
        remote = [
            pltpu.make_async_remote_copy(
                src_ref=dctx_stage.at[t, where],
                dst_ref=dctx_far.at[place, pl.ds(t * SUBS, SUBS)],
                send_sem=send.at[t, n],
                recv_sem=recv.at[t, n],
                device_id=other,
                device_id_type=MESH,
            )
            for n, (where, other) in enumerate(others)
        ]
        swap = pltpu.make_async_remote_copy(
            src_ref=out_stage.at[t],
            dst_ref=out_far.at[t],
            send_sem=send.at[t, 3],
            recv_sem=recv.at[t, 3],
            device_id=me.by_swap,
            device_id_type=MESH,
        )
        keep = pltpu.make_async_copy(out_stage.at[t], out_far.at[t], local.at[t, 0])
        own = pltpu.make_async_copy(
            dctx_stage.at[t, place], dctx_far.at[place, pl.ds(t * SUBS, SUBS)], local.at[t, 1]
        )
        return remote, own, swap, keep

    @pl.when(step == 0)
    def _():
        for g in range(groups):
            wop_ref[g * LANES : (g + 1) * LANES, :] = wo_ref[g * wide : g * wide + LANES, :]
            to = groups * LANES + g * HEAD_DIM
            wop_ref[to : to + HEAD_DIM, :] = wo_ref[g * wide + LANES : (g + 1) * wide, :]
        gvec_ref[...] = jnp.zeros_like(gvec_ref)
        gbu_ref[...] = jnp.zeros_like(gbu_ref)

    low = lax.broadcasted_iota(jnp.int32, (BLOCK, LANES), 1) < HEAD_DIM
    subs = range(tok_ref.shape[0] // ROWS)
    spans = [slice(n * ROWS, (n + 1) * ROWS) for n in subs]
    chunks = [slice(f, f + CHUNK) for f in range(0, hidden, CHUNK)]
    for n in subs:
        for g in range(groups):
            mix_ref[spans[n], g * LANES : (g + 1) * LANES] = ctx_ref[g, n, :ROWS, :]
        for g in range(0, groups, 2):
            to = groups * LANES + g * HEAD_DIM
            for m in range(ROWS // (2 * BLOCK)):
                at = ROWS + m * BLOCK
                a = ctx_ref[g, n, at : at + BLOCK, :].astype(f32)
                b = ctx_ref[g + 1, n, at : at + BLOCK, :].astype(f32)
                even = jnp.where(low, a, pltpu.roll(b, HEAD_DIM, 1))
                odd = jnp.where(low, pltpu.roll(a, HEAD_DIM, 1), b)
                r = n * ROWS + 2 * m * BLOCK
                mix_ref[r : r + BLOCK, to : to + LANES] = even.astype(bf16)
                mix_ref[r + BLOCK : r + 2 * BLOCK, to : to + LANES] = odd.astype(bf16)

    bo, g1, s1 = vec_ref[0:1, :], vec_ref[1:2, :], vec_ref[2:3, :]
    bd, g2, s2 = vec_ref[3:4, :], vec_ref[4:5, :], vec_ref[5:6, :]
    projs = [dot(mix_ref[rows, :], wop_ref[...]) for rows in spans]
    norms = [norm(tok_ref[rows, :].astype(f32) + proj + bo) for rows, proj in zip(spans, projs)]
    hids = [n1 * g1 + s1 for n1, _ in norms]
    lows = [hid.astype(bf16) for hid in hids]
    for rows, hid_low in zip(spans, lows):
        hid_ref[rows, :] = hid_low
    scale = np.sqrt(2.0 / np.pi).astype(np.float32)
    work = [(n, cols) for cols in chunks for n in subs]

    def behind(start, end):
        held = start(*work[0])
        for k, item in enumerate(work):
            now = held
            if k + 1 < len(work):
                held = start(*work[k + 1])
            end(*item, now)

    def up_start(n, cols):
        return dot(lows[n], wu_ref[:, cols])

    def up_end(n, cols, raw):
        u = raw + bu_ref[:, cols]
        square = u * u
        t = jnp.tanh(u * (scale + (scale * 0.044715) * square))
        half = 0.5 + 0.5 * t
        act_ref[spans[n], cols] = (u * half).astype(bf16)
        slope = half + (0.5 * u) * (1.0 - t * t) * (scale + (3 * 0.044715 * scale) * square)
        slope_ref[spans[n], cols] = slope.astype(bf16)

    behind(up_start, up_end)
    ffns = [dot(act_ref[rows, :], wd_ref[...]) for rows in spans]
    dres2s, dffns = [], []
    for n, rows in enumerate(spans):
        n2, rstd2 = norm(hids[n] + ffns[n] + bd)
        out_ref[rows, :] = (n2 * g2 + s2).astype(bf16)
        og = og_ref[rows, :].astype(f32)
        gvec_ref[4:5, :] += rowsum(og * n2)
        gvec_ref[5:6, :] += rowsum(og)
        dres2 = norm_back(og * g2, n2, rstd2)
        dffn = dres2.astype(bf16)
        dffn_ref[rows, :] = dffn
        gvec_ref[3:4, :] += rowsum(dffn.astype(f32))
        dres2s.append(dres2)
        dffns.append(dffn)

    if direct:
        remote, own, swap, keep = transfers(step)

        @pl.when(me.stays)
        def _():
            keep.start()

        @pl.when(jnp.logical_not(me.stays))
        def _():
            swap.start()

    def down_start(n, cols):
        return dot_nt(dffns[n], wd_ref[cols, :])

    def down_end(n, cols, dact):
        dpre = (dact * slope_ref[spans[n], cols].astype(f32)).astype(bf16)
        dpre_ref[spans[n], cols] = dpre
        gbu_ref[0:1, cols] += rowsum(dpre.astype(f32))

    behind(down_start, down_end)
    dhs = [dres2 + dot_nt(dpre_ref[rows, :], wu_ref[...]) for rows, dres2 in zip(spans, dres2s)]
    dmixes = []
    for rows, dh, (n1, rstd1) in zip(spans, dhs, norms):
        gvec_ref[1:2, :] += rowsum(dh * n1)
        gvec_ref[2:3, :] += rowsum(dh)
        dres1 = norm_back(dh * g1, n1, rstd1)
        dres_ref[rows, :] = dres1
        dproj = dres1.astype(bf16)
        dproj_ref[rows, :] = dproj
        gvec_ref[0:1, :] += rowsum(dproj.astype(f32))
        dmixes.append(dot_nt(dproj, wop_ref[...]))
    for n, dmix in enumerate(dmixes):
        for g in range(groups):
            dctx_ref[g, n, :ROWS, :] = dmix[:, g * LANES : (g + 1) * LANES].astype(bf16)
        for g in range(0, groups, 2):
            to = groups * LANES + g * HEAD_DIM
            for m in range(ROWS // (2 * BLOCK)):
                at = ROWS + m * BLOCK
                r = 2 * m * BLOCK
                even = dmix[r : r + BLOCK, to : to + LANES]
                odd = dmix[r + BLOCK : r + 2 * BLOCK, to : to + LANES]
                a = jnp.where(low, even, pltpu.roll(odd, HEAD_DIM, 1))
                b = jnp.where(low, pltpu.roll(even, HEAD_DIM, 1), odd)
                dctx_ref[g, n, at : at + BLOCK, :] = a.astype(bf16)
                dctx_ref[g + 1, n, at : at + BLOCK, :] = b.astype(bf16)

    if direct:
        for copy in remote:
            copy.start()
        own.start()

        @pl.when(step == pl.num_programs(0) - 1)
        def _():
            for t in range(dctx_stage.shape[0]):
                remote, own, swap, keep = transfers(t)
                for copy in remote:
                    copy.wait()
                own.wait()

                @pl.when(me.stays)
                def _():
                    keep.wait()

                @pl.when(jnp.logical_not(me.stays))
                def _():
                    swap.wait()


def chain(ctx, tok, og, wo, wu, wd, vec, bu, direct):
    rows, width = tok.shape
    hidden = wu.shape[1]
    groups = ctx.shape[0]
    once = pl.Buffered(1)

    def tiled(cols):
        return pl.BlockSpec((SUBS * ROWS, cols), lambda t: (t, 0))

    def fixed(shape):
        return pl.BlockSpec(shape, lambda t: (0, 0), pipeline_mode=once)

    packed = pl.BlockSpec((groups, SUBS) + ctx.shape[2:], lambda t: (0, t, 0, 0))
    shape = jax.ShapeDtypeStruct
    steps = rows // (SUBS * ROWS)
    hbm = pl.BlockSpec(memory_space=pltpu.HBM)
    scratch = [pltpu.VMEM((SUBS * ROWS, hidden), bf16), pltpu.VMEM(wo.shape, bf16)]
    params = pltpu.CompilerParams(vmem_limit_bytes=VMEM_BYTES)
    out_shape = (rows, width)
    if direct:
        out_shape = (steps, SUBS * ROWS, width)
        scratch += [
            pltpu.VMEM(out_shape, bf16),
            pltpu.VMEM((steps, groups, SUBS) + ctx.shape[2:], bf16),
            pltpu.SemaphoreType.DMA((steps, 4)),
            pltpu.SemaphoreType.DMA((steps, 4)),
            pltpu.SemaphoreType.DMA((steps, 2)),
        ]
        params = pltpu.CompilerParams(
            vmem_limit_bytes=VMEM_BYTES, collective_id=2, has_side_effects=True
        )
    return pl.pallas_call(
        partial(chain_kernel, groups, direct),
        grid=(steps,),
        out_shape=(
            shape(out_shape, bf16),
            shape((rows, width), f32),
            shape(ctx.shape, bf16),
            shape((rows, width), bf16),
            shape((rows, width), bf16),
            shape((rows, hidden), bf16),
            shape((rows, hidden), bf16),
            shape((rows, width), bf16),
            shape((rows, width), bf16),
            shape((8, width), f32),
            shape((8, hidden), f32),
        ),
        in_specs=[
            packed,
            tiled(width),
            tiled(width),
            fixed(wo.shape),
            fixed(wu.shape),
            fixed(wd.shape),
            fixed(vec.shape),
            fixed(bu.shape),
        ],
        out_specs=(
            hbm if direct else tiled(width),
            tiled(width),
            hbm if direct else packed,
            tiled(width),
            tiled(width),
            tiled(hidden),
            tiled(hidden),
            tiled(width),
            tiled(width),
            pl.BlockSpec((8, width), lambda t: (0, 0)),
            pl.BlockSpec((8, hidden), lambda t: (0, 0)),
        ),
        scratch_shapes=scratch,
        compiler_params=params,
        name="chain",
    )(ctx, tok, og, wo, wu, wd, vec, bu)


def gather_item(me, copies, shard, full, cols, x_first):
    y, x, core, zh, zl = me.y, me.x, me.core, me.zh, me.zl
    mine = shard.at[:, cols]
    own = copies.local(mine, full.at[y, x, core, me.z, :, cols])
    spot = full.at[y, x, core, me.z, :, cols]
    along = [copies.remote(mine, spot, other) for other in (me.by_zl, me.by_mid, me.by_zh)]
    own.start()
    for copy in along:
        copy.start()
    yield 1
    own.wait()
    for copy in along:
        copy.wait()
    line = full.at[y, x, core, :, :, cols]
    near = copies.remote(line, line, me.by_x if x_first else me.by_y)
    near.start()
    across = [copies.remote(line, line, me.by_core)]
    across[0].start()
    yield 1
    near.wait()
    if x_first:
        block = full.at[y, :, core, :, :, cols]
        got = full.at[y, 1 - x, core, :, :, cols]
        rest = full.at[1 - y, :, core, :, :, cols]
    else:
        block = full.at[:, x, core, :, :, cols]
        got = full.at[1 - y, x, core, :, :, cols]
        rest = full.at[:, 1 - x, core, :, :, cols]
    far = copies.remote(block, block, me.by_y if x_first else me.by_x)
    far.start()
    across.append(copies.remote(got, got, me.by_core))
    across[1].start()
    yield 1
    far.wait()
    across.append(copies.remote(rest, rest, me.by_core))
    across[2].start()
    yield 1
    for copy in across:
        copy.wait()


def tokens_item(me, copies, tok, x_all, piece):
    place = me.core * 2 + me.zl
    there = (1 - me.core) * 2 + me.zl
    held = x_all.at[place, piece]
    out = copies.remote(tok.at[piece], x_all.at[there, piece], me.by_swap)
    keep = copies.local(tok.at[piece], held)
    along = copies.remote(held, held, me.by_zl)
    over = copies.remote(held, held, me.by_core)

    @pl.when(me.stays)
    def _():
        keep.start()

    @pl.when(jnp.logical_not(me.stays))
    def _():
        out.start()

    yield 1

    @pl.when(me.stays)
    def _():
        keep.wait()
        along.start()
        over.start()

    yield 1

    @pl.when(jnp.logical_not(me.stays))
    def _():
        out.wait()
        along.start()
        over.start()

    yield 1
    along.wait()
    came = x_all.at[me.core * 2 + 1 - me.zl, piece]
    onto = copies.remote(came, came, me.by_core)
    onto.start()
    yield 1
    over.wait()
    onto.wait()


def exchange_item(me, copies, src, dst):
    out = copies.remote(src, dst, me.by_swap)
    keep = copies.local(src, dst)

    @pl.when(me.stays)
    def _():
        keep.start()

    @pl.when(jnp.logical_not(me.stays))
    def _():
        out.start()

    yield 1

    @pl.when(me.stays)
    def _():
        keep.wait()

    @pl.when(jnp.logical_not(me.stays))
    def _():
        out.wait()


PIECES = 4


def weight_item(me, copies, src, parts, whole, bias):
    y, x, core, zh, zl = me.y, me.x, me.core, me.zh, me.zl
    place = core * 2 + zl
    keep = copies.local(src.at[place], parts.at[place])
    moves = [
        copies.remote(src.at[core * 2 + 1 - zl], parts.at[place], me.by_zl),
        copies.remote(src.at[(1 - core) * 2 + zl], parts.at[place], me.by_core),
        copies.remote(src.at[(1 - core) * 2 + 1 - zl], parts.at[place], me.by_both),
    ]
    keep.start()
    for move in moves:
        move.start()
    yield 1
    keep.wait()
    for move in moves:
        move.wait()
    own = whole.shape[4] // 2
    for b in range(2):
        both = jnp.concatenate([parts[2 * b, :own, :], parts[2 * b + 1, :own, :]], axis=0)
        whole[y, x, b, zh] = both.astype(bf16)
    tail = pl.ds(own, 8)
    bias[y, x, zh] = parts[0, tail, :] + parts[1, tail, :] + parts[2, tail, :] + parts[3, tail, :]
    for spot, bias_spot, other in (
        (whole.at[y, x, :, zh], bias.at[y, x, zh], me.by_zh),
        (whole.at[y, x], bias.at[y, x], me.by_x),
        (whole.at[y], bias.at[y], me.by_y),
    ):
        moves = [copies.remote(spot, spot, other), copies.remote(bias_spot, bias_spot, other)]
        for move in moves:
            move.start()
        yield 1
        for move in moves:
            move.wait()


def finish(*generators):
    for phases in generators:
        for _ in phases:
            pass


def front_kernel(heads, randoms, *refs):
    rand_ref, tok, og, wq, w_out, up, down, small = refs[:8]
    x_hbm, tok_own, og_own, w_own, qkv_hbm, res_hbm, ctx_all, out_all, up_all, down_all, small_all = refs[8:19]
    x_all, parts, whole, bias, qkv_ref, res_ref, ends_ref, ctx_ref = refs[19:27]
    me = Where()
    me.greet()
    copies = Copies(*refs[27:])
    blocks = qkv_ref.shape[0]
    length = blocks * BLOCK
    quarter = length // 4
    core, zl = me.core, me.zl
    place = core * 2 + zl
    near = core * 2 + 1 - zl
    beside = (1 - core) * 2 + zl
    across = (1 - core) * 2 + 1 - zl

    weights = weight_item(me, copies, wq, parts, whole, bias)
    tokens = [tokens_item(me, copies, tok, x_all, piece) for piece in range(PIECES)]
    smalls = gather_item(me, copies, small, small_all, slice(0, LANES), True)
    turn = 0

    def gathers(*arrays):
        nonlocal turn
        made = []
        for shard, full, splits in arrays:
            width = shard.shape[1] // splits
            for n in range(splits):
                cols = slice(n * width, (n + 1) * width)
                made.append(gather_item(me, copies, shard, full, cols, turn % 2 == 0))
                turn += 1
        return made

    def advance(group):
        group[:] = [phases for phases in group if next(phases, None) is not None]

    early = gathers((up, up_all, 2))
    late = gathers((down, down_all, 2), (w_out, out_all, 2))
    last = [exchange_item(me, copies, og.at[n], og_own.at[n]) for n in range(PIECES)]
    idle = [smalls]
    outs = []

    def write(src, dst):
        copy = copies.local(src, dst)
        copy.start()
        outs.append(copy)

    def project(where):
        bias_row = jnp.sum(bias[...].reshape(-1, 8, bias.shape[-1]), axis=0)[0:1]
        matrix = whole[...].reshape(-1, whole.shape[-1])
        for piece in range(PIECES):
            raw = dot(x_all[where, piece], matrix) + bias_row
            step = ROWS // BLOCK
            at = (where * PIECES + piece) * step
            qkv_ref[pl.ds(at, step)] = raw.astype(bf16).reshape(step, BLOCK, raw.shape[1])

    def forward_tokens():
        for item in tokens:
            next(item)

    next(weights)
    advance(early)
    next(weights)
    forward_tokens()
    forward_tokens()
    next(weights)
    advance(idle)
    advance(early)
    next(weights)
    advance(idle)
    forward_tokens()
    advance(late)
    finish(weights)
    advance(early)
    next(last[0])
    project(place)
    write(whole, w_own)
    write(x_all.at[place], tok_own)
    forward_tokens()
    advance(late)
    next(last[1])
    project(near)
    finish(*tokens)
    next(last[2])
    next(last[3])
    advance(early)
    project(beside)
    project(across)
    advance(idle)
    write(x_all, x_hbm)
    write(qkv_ref, qkv_hbm)
    for h, both in enumerate(global_blocks(qkv_ref, heads, length)):
        ends_ref[h] = both
    advance(late)
    advance(early)
    advance(idle)

    def middle(t, carry):
        middle_blocks(qkv_ref, rand_ref, res_ref, t * PAIR, heads, randoms, blocks)
        return carry

    sends = []
    turns = quarter // BLOCK // PAIR
    for where, other in ((across, me.by_both), (near, me.by_zl), (beside, me.by_core), (place, None)):
        lax.fori_loop(where * turns, (where + 1) * turns, middle, 0)

        @pl.when(where == 0)
        def _():
            for h in range(heads):
                res_ref[h, 0:BLOCK, :] = ends_ref[h, 0:BLOCK, :]

        @pl.when(where == 3)
        def _():
            for h in range(heads):
                res_ref[h, length - BLOCK : length, :] = ends_ref[h, BLOCK : 2 * BLOCK, :]

        for piece in range(PIECES):
            pack_rows(res_ref, ctx_ref, where * quarter + piece * ROWS, where, piece)
        rows = rows_at(where * quarter, quarter)
        write(res_ref.at[:, rows], res_hbm.at[:, rows])
        if other is None:
            write(ctx_ref.at[where], ctx_all.at[place])
        else:
            send = copies.remote(ctx_ref.at[where], ctx_all.at[place], other)
            send.start()
            sends.append(send)
        advance(late if where is near or where is place else idle)
    finish(*early, *late, *last, *idle)
    for copy in sends + outs:
        copy.wait()


def front(rand, tok, og, wq, mats, small, heads):
    rows, width = tok.shape
    members = 4
    length = rows * members
    randoms = rand.size // (heads * (length // BLOCK - 2))
    hbm = pl.BlockSpec(memory_space=pltpu.HBM)
    shape = jax.ShapeDtypeStruct
    tok = tok.reshape(PIECES, rows // PIECES, width)
    og = og.reshape(tok.shape)
    cols = heads * SLOT
    own = mats[0].shape[0]
    packed = (members, rows // ROWS, ROWS * 3 // 2, LANES)
    outs = [
        shape((members,) + tok.shape, bf16),
        shape(tok.shape, bf16),
        shape(og.shape, bf16),
        shape((2, 2, 2, 2, 2 * own, cols), bf16),
        shape((length // BLOCK, BLOCK, cols), bf16),
        shape((heads, length, LANES), f32),
        shape(packed, bf16),
    ]
    outs += [shape((2, 2, 2, 4) + a.shape, bf16) for a in (*mats, small)]
    return pl.pallas_call(
        partial(front_kernel, heads, randoms),
        out_shape=tuple(outs),
        in_specs=[pl.BlockSpec(memory_space=pltpu.SMEM)] + [hbm] * 7,
        out_specs=(hbm,) * 11,
        scratch_shapes=[
            pltpu.VMEM((members,) + tok.shape, bf16),
            pltpu.VMEM(wq.shape, f32),
            pltpu.VMEM((2, 2, 2, 2, 2 * own, cols), bf16),
            pltpu.VMEM((2, 2, 2, 8, cols), f32),
            pltpu.VMEM((length // BLOCK, BLOCK, cols), bf16),
            pltpu.VMEM((heads, length, LANES), f32),
            pltpu.VMEM((heads, 2 * BLOCK, LANES), f32),
            pltpu.VMEM(packed, bf16),
            pltpu.SemaphoreType.DMA((112,)),
            pltpu.SemaphoreType.DMA((112,)),
            pltpu.SemaphoreType.DMA((32,)),
        ],
        compiler_params=pltpu.CompilerParams(
            collective_id=0, has_side_effects=True, vmem_limit_bytes=VMEM_BYTES
        ),
        name="front",
    )(rand, tok, og, wq, *mats, small)


def add_rows(dst, a, b, rows):
    step = next(n for n in (48, 32, 24, 16, 8) if rows % n == 0)

    def body(t, carry):
        at = rows_at(t * step, step)
        dst[at, :] = (a[at, :].astype(f32) + b[at, :].astype(f32)).astype(dst.dtype)
        return carry

    lax.fori_loop(0, rows // step, body, 0)


def scatter_item(me, copies, src, cols, acc, from_core, from_first, from_second, slabs, from_line, out, x_first):
    y, x, core, zh, zl = me.y, me.x, me.core, me.zh, me.zl
    rows = acc.shape[2]
    own = None
    if cols is not None:
        own = copies.local(src.at[:, :, core, :, cols], acc)
        own.start()
        src = src.at[:, :, 1 - core, :, cols]
    over = copies.remote(src, from_core, me.by_core)
    over.start()
    yield 1
    if own is not None:
        own.wait()
    over.wait()
    for a in range(2):
        for b in range(2):
            add_rows(acc.at[a, b], acc.at[a, b], from_core.at[a, b], rows)
    if x_first:
        first = copies.remote(acc.at[:, 1 - x], from_first, me.by_x)
    else:
        first = copies.remote(acc.at[1 - y], from_first, me.by_y)
    first.start()
    yield 1
    first.wait()
    for a in range(2):
        block = acc.at[a, x] if x_first else acc.at[y, a]
        add_rows(block, block, from_first.at[a], rows)
    if x_first:
        second = copies.remote(acc.at[1 - y, x], from_second, me.by_y)
    else:
        second = copies.remote(acc.at[y, 1 - x], from_second, me.by_x)
    second.start()
    yield 1
    second.wait()
    rest = rows // 4
    summed = acc[y, x].astype(f32) + from_second[...].astype(f32)
    for z in range(4):
        slabs[z] = summed[z * rest : (z + 1) * rest].astype(slabs.dtype)
    moves = [
        copies.remote(slabs.at[(1 - zh) * 2 + zl], from_line.at[0], me.by_zh),
        copies.remote(slabs.at[(1 - zh) * 2 + 1 - zl], from_line.at[1], me.by_mid),
        copies.remote(slabs.at[zh * 2 + 1 - zl], from_line.at[2], me.by_zl),
    ]
    for move in moves:
        move.start()
    yield 1
    for move in moves:
        move.wait()
    near = slabs[me.z].astype(f32) + from_line[2].astype(f32)
    out[...] = near + (from_line[0].astype(f32) + from_line[1].astype(f32))


def scatter_buffers(rows, cols, kind):
    return [
        pltpu.VMEM((2, 2, rows, cols), kind),
        pltpu.VMEM((2, 2, rows, cols), kind),
        pltpu.VMEM((2, rows, cols), kind),
        pltpu.VMEM((rows, cols), kind),
        pltpu.VMEM((4, rows // 4, cols), kind),
        pltpu.VMEM((3, rows // 4, cols), kind),
    ]


def own_columns_item(me, copies, acc, from_x, from_y, from_zh, part, blocks, out):
    y, x, core, zh, zl = me.y, me.x, me.core, me.zh, me.zl
    rows = acc.shape[4]
    first = copies.remote(acc.at[1 - x], from_x, me.by_x)
    first.start()
    yield 1
    first.wait()
    for a in range(2):
        for b in range(2):
            for c in range(2):
                add_rows(acc.at[x, a, b, c], acc.at[x, a, b, c], from_x.at[a, b, c], rows)
    acc = acc.at[x]
    second = copies.remote(acc.at[1 - y], from_y, me.by_y)
    second.start()
    yield 1
    second.wait()
    for b in range(2):
        for c in range(2):
            block = acc.at[y, b, c]
            add_rows(block, block, from_y.at[b, c], rows)
    third = copies.remote(acc.at[y, :, 1 - zh], from_zh, me.by_zh)
    third.start()
    yield 1
    third.wait()
    half = rows // 2
    for b in range(2):
        add_rows(part.at[b], acc.at[y, b, zh], from_zh.at[b], rows)
    place = core * 2 + zl
    mine = rows_at(zl * half, half)
    other = rows_at((1 - zl) * half, half)
    keep = copies.local(part.at[core, mine], blocks.at[place])
    keep.start()
    moves = [
        copies.remote(part.at[core, other], blocks.at[place], me.by_zl),
        copies.remote(part.at[1 - core, mine], blocks.at[place], me.by_core),
        copies.remote(part.at[1 - core, other], blocks.at[place], me.by_both),
    ]
    for move in moves:
        move.start()
    yield 1
    keep.wait()
    for move in moves:
        move.wait()
    heads = blocks.shape[2] // SLOT
    low = lax.broadcasted_iota(jnp.int32, (blocks.shape[1], LANES), 1) < HEAD_DIM
    for kind in range(3):
        for n in range(0, 4 * heads, 2):
            pair = []
            for head in (n, n + 1):
                at = head % heads * SLOT + (0 if kind == 0 else LANES)
                pair.append(blocks[head // heads, :, at : at + LANES])
            if kind == 2:
                tile = jnp.where(low, pltpu.roll(pair[0], HEAD_DIM, 1), pair[1])
            else:
                tile = jnp.where(low, pair[0], pltpu.roll(pair[1], HEAD_DIM, 1))
            if kind == 0:
                tile = tile * HEAD_DIM**-0.5
            to = (kind * 4 * heads + n) * HEAD_DIM
            out[:, to : to + LANES] = tile


def input_grad_item(me, copies, draw, w, dres, piece, stage, from_core, from_zl, res, out):
    core, zl = me.core, me.zl
    more = copies.local(dres.at[piece], res)
    more.start()
    for b in range(2):
        stage[b] = dot_nt(draw[(1 - core) * 2 + b, piece], w[...]).astype(bf16)
    over = copies.remote(stage, from_core, me.by_core)
    over.start()
    yield 1
    mine = dot_nt(draw[core * 2 + 1 - zl, piece], w[...])
    over.wait()
    far, send = stage.at[0], stage.at[1]
    far[...] = (mine + from_core[1 - zl].astype(f32)).astype(bf16)
    along = copies.remote(far, from_zl, me.by_zl)
    along.start()
    mine = dot_nt(draw[core * 2 + zl, piece], w[...])
    more.wait()
    res[...] = res[...] + (mine + from_core[zl].astype(f32))
    yield 1
    along.wait()
    send[...] = (res[...] + from_zl[...].astype(f32)).astype(bf16)
    yield from exchange_item(me, copies, send, out.at[piece])


def scatter_kernel(*refs):
    act, dffn, hid, dpre, proj, vecs, draw, x_hbm, w, dres = refs[:10]
    outs = refs[10:16]
    sems, scratch = refs[16:19], list(refs[19:])
    me = Where()
    me.greet()
    copies = Copies(*sems)

    def take(n):
        got = scratch[:n]
        del scratch[:n]
        return got

    def advance(group):
        group[:] = [phases for phases in group if next(phases, None) is not None]

    pieces = [
        input_grad_item(me, copies, draw, w, dres, piece, *take(4), outs[5]) for piece in range(PIECES)
    ]
    x_all, total, acc, *buffers = take(8)
    columns = [own_columns_item(me, copies, acc, *buffers, outs[4])]
    halves, quarters, stage_down, stage_up = take(4)
    first, second = [], []
    for n in range(2):
        cols = outs[0].shape[1] // 2
        part = outs[0].at[:, n * cols : (n + 1) * cols]
        first.append(
            scatter_item(me, copies, stage_down.at[n], None, halves.at[n], *take(5), part, n % 2 == 0)
        )
    for n in range(4):
        cols = outs[1].shape[1] // 4
        part = outs[1].at[:, n * cols : (n + 1) * cols]
        second.append(
            scatter_item(me, copies, stage_up.at[n], None, quarters.at[n], *take(5), part, n % 2 == 0)
        )
    for src, out, group in ((proj, outs[2], first), (vecs, outs[3], second)):
        whole = slice(0, src.shape[4])
        group.append(scatter_item(me, copies, src, whole, *take(6), out, True))

    def fetch(src):
        wide = x_all.shape[3]
        got = [copies.local(src.at[:, :, c * wide : (c + 1) * wide], x_all.at[c]) for c in range(4)]
        for copy in got:
            copy.start()
        return got

    def flat(value):
        return value.reshape(-1, value.shape[-1])

    def down_grad(c, carry):
        g = dot_tn(flat(x_all[c]), flat(dffn[...])).astype(bf16)
        rows, cols = g.shape[0] // 2, g.shape[1] // 2
        for n in range(2):
            low, high = g[:rows, n * cols : (n + 1) * cols], g[rows:, n * cols : (n + 1) * cols]
            halves[n, c // 2, c % 2] = jnp.where(me.core == 0, low, high)
            stage_down[n, c // 2, c % 2] = jnp.where(me.core == 0, high, low)
        return carry

    def up_grad(c, carry):
        g = dot_tn(flat(hid[...]), flat(x_all[c])).astype(bf16)
        rows = g.shape[0] // 8
        for k in range(4):
            low, high = g[2 * k * rows : (2 * k + 1) * rows], g[(2 * k + 1) * rows : (2 * k + 2) * rows]
            quarters[c, k // 2, k % 2] = jnp.where(me.core == 0, low, high)
            stage_up[c, k // 2, k % 2] = jnp.where(me.core == 0, high, low)
        return carry

    def weight_grad(t, carry):
        place, piece = t // PIECES, t % PIECES
        total[...] += dot_tn(x_all[place, piece], draw[place, piece])
        return carry

    got = fetch(act)
    next(pieces[0])
    next(pieces[1])
    next(pieces[0])
    next(pieces[1])
    for copy in got:
        copy.wait()
    lax.fori_loop(0, 4, down_grad, 0)
    got = fetch(dpre)
    advance(first)
    next(pieces[2])
    next(pieces[3])
    next(pieces[2])
    next(pieces[3])
    for copy in got:
        copy.wait()
    advance(first)
    lax.fori_loop(0, 4, up_grad, 0)
    got = copies.local(x_hbm, x_all)
    got.start()
    advance(second)
    next(pieces[0])
    total[...] = jnp.zeros_like(total)
    got.wait()
    advance(second)
    next(pieces[1])
    lax.fori_loop(0, 2 * PIECES, weight_grad, 0)
    next(pieces[2])
    advance(first)
    lax.fori_loop(2 * PIECES, 4 * PIECES, weight_grad, 0)
    laid = total[...].reshape((2, 2) + acc.shape[2:])
    for a in range(2):
        for b in range(2):
            acc[b, a] = laid[a, b].astype(bf16)
    advance(columns)
    next(pieces[3])
    advance(first)
    advance(second)
    while pieces or columns or first or second:
        advance(columns)
        advance(second)
        advance(first)
        if not second:
            advance(pieces)


def scatter(act, dffn, hid, dpre, proj, vecs, draw, x_all, w, dres, own):
    hbm = pl.BlockSpec(memory_space=pltpu.HBM)
    vmem = pl.BlockSpec(memory_space=pltpu.VMEM)
    shape = jax.ShapeDtypeStruct
    hidden = act.shape[-1]
    outs = [shape((hidden // 32, w.shape[0]), f32), shape((own, hidden), f32)]
    outs += [shape((a.shape[3] // 4, a.shape[4]), f32) for a in (proj, vecs)]
    width, cols = w.shape
    rows = 2 * own
    outs.append(shape((own, 3 * cols), f32))
    outs.append(shape(dres.shape, bf16))
    buffers = []
    for _ in range(PIECES):
        tile = dres.shape[1:]
        buffers += [
            pltpu.VMEM((2,) + tile, bf16),
            pltpu.VMEM((2,) + tile, bf16),
            pltpu.VMEM(tile, bf16),
            pltpu.VMEM(tile, f32),
        ]
    buffers += [
        pltpu.VMEM(x_all.shape, bf16),
        pltpu.VMEM((width, cols), f32),
        pltpu.VMEM((2, 2, 2, 2, rows, cols), bf16),
        pltpu.VMEM((2, 2, 2, rows, cols), bf16),
        pltpu.VMEM((2, 2, rows, cols), bf16),
        pltpu.VMEM((2, rows, cols), bf16),
        pltpu.VMEM((2, rows, cols), f32),
        pltpu.VMEM((4, own, cols), f32),
    ]
    down = (hidden // 8, width // 2)
    up = (4 * own, hidden // 4)
    buffers += [
        pltpu.VMEM((2, 2, 2) + down, bf16),
        pltpu.VMEM((4, 2, 2) + up, bf16),
        pltpu.VMEM((2, 2, 2) + down, bf16),
        pltpu.VMEM((4, 2, 2) + up, bf16),
    ]
    for tile in [down] * 2 + [up] * 4:
        buffers += scatter_buffers(*tile, bf16)[1:]
    for a in (proj, vecs):
        buffers += scatter_buffers(*a.shape[3:], a.dtype)
    return pl.pallas_call(
        scatter_kernel,
        out_shape=tuple(outs),
        in_specs=[hbm, vmem, vmem, hbm, hbm, hbm, vmem, hbm, vmem, hbm],
        out_specs=(vmem,) * 5 + (hbm,),
        scratch_shapes=[
            pltpu.SemaphoreType.DMA((80,)),
            pltpu.SemaphoreType.DMA((80,)),
            pltpu.SemaphoreType.DMA((32,)),
        ]
        + buffers,
        compiler_params=pltpu.CompilerParams(
            collective_id=1, has_side_effects=True, vmem_limit_bytes=VMEM_BYTES
        ),
        name="scatter",
    )(act, dffn, hid, dpre, proj, vecs, draw, x_all, w, dres)


def per_device(
    tokens,
    qkv_weight,
    query_value_bias,
    out_weight,
    out_bias,
    norm1_gain,
    norm1_bias,
    up_weight,
    up_bias,
    down_weight,
    down_bias,
    norm2_gain,
    norm2_bias,
    rand_blocks,
    out_grad,
):
    members = lax.axis_size(GROUP)
    devices = lax.axis_size(ALL)
    swap = [(0, 0), (1, 2), (2, 1), (3, 3)]

    def move(a):
        return lax.ppermute(a, ("core", "zh"), swap)

    rand = move(rand_blocks[0])
    heads = rand.shape[0]
    rows, width = tokens.shape[1:]
    cols = heads * HEAD_DIM
    group = lax.axis_index(GROUP)
    own = width // devices
    rand_flat = rand.reshape(-1)

    def lay_out(a):
        a = a.reshape(a.shape[:-2] + (3, heads, HEAD_DIM))
        q, k, v = a[..., 0, :, :], a[..., 1, :, :], a[..., 2, :, :]
        q = q * jnp.asarray(HEAD_DIM**-0.5, a.dtype)
        laid = jnp.stack([q, jnp.zeros_like(q), k, v], axis=-2)
        return laid.reshape(laid.shape[:-3] + (heads * SLOT,))

    bias_part = jnp.stack([query_value_bias[0], jnp.zeros((own,), bf16), query_value_bias[1]])
    small = [out_bias, norm1_gain, norm1_bias, down_bias, norm2_gain, norm2_bias, up_bias]
    small = jnp.concatenate(small)
    direct = lax.axis_size("c") == 4 and members == 4 and own % 8 == 0
    if direct:
        count = small.shape[0]
        padded = jnp.pad(small, (0, 16 * LANES - count)).reshape(16, LANES)
        spread = lax.dynamic_update_slice(
            jnp.zeros((3, width), f32), bias_part.astype(f32), (0, lax.axis_index(ALL) * own)
        )
        spread = lay_out(jnp.transpose(spread.reshape(3, members, cols), (1, 0, 2)))
        wq = jnp.transpose(qkv_weight.astype(f32).reshape(own, 3, members, cols), (2, 0, 1, 3))
        wq = jnp.concatenate([lay_out(wq), spread[:, None], jnp.zeros((members, 7, heads * SLOT), f32)], axis=1)
        mats = (out_weight, up_weight, down_weight)
        x, tok, og, w_own, qkv, res, ctx, *full = front(
            rand_flat, tokens[0], out_grad[0], wq, mats, padded, heads
        )
        x, tok, og = (a.reshape(-1, width) for a in (x, tok, og))
        w_own = w_own.reshape(width, -1)
        w_out, w_up, w_down = (a.reshape(-1, a.shape[-1]) for a in full[:3])
        small = full[3].reshape(devices, -1)[:, :count].astype(f32)
    else:
        tok = move(tokens[0])
        og = move(out_grad[0])
        x = lax.all_gather(tok, GROUP, axis=0, tiled=True)
        mats = (qkv_weight, out_weight, up_weight, down_weight)
        w_qkv, w_out, w_up, w_down = (lax.all_gather(a, ALL, axis=0, tiled=True) for a in mats)
        small = lax.all_gather(small, ALL, axis=0).astype(f32)
        w_own = lax.dynamic_slice_in_dim(
            w_qkv.reshape(width, 3, members, cols), group, 1, axis=2
        ).reshape(width, 3, cols)
        w_own = lay_out(w_own)
        bias3 = lax.all_gather(bias_part, ALL, axis=1, tiled=True).astype(f32).reshape(3, members, cols)
        b_own = lay_out(lax.dynamic_slice_in_dim(bias3, group, 1, axis=1).reshape(1, 3, cols))
        qkv, res, ctx_send = attend(rand_flat, x, w_own, b_own, members, heads)
        ctx = lax.all_to_all(ctx_send, GROUP, split_axis=0, concat_axis=0, tiled=True)
    vecs = jnp.transpose(small[:, : 6 * own].reshape(devices, 6, own), (1, 0, 2)).reshape(6, width)
    bias_up = small[:, 6 * own :].reshape(1, -1)
    chain_vecs = jnp.concatenate([vecs, jnp.zeros((2, width), f32)], axis=0)
    out, dres1, dctx, mix, hid, act, dpre, dffn, dproj, gvec, gbu = chain(
        ctx, tok, og, w_out, w_up, w_down, chain_vecs, bias_up, direct
    )
    if direct:
        out = out.reshape(rows, width)
    else:
        dctx = lax.all_to_all(dctx, GROUP, split_axis=0, concat_axis=0, tiled=True)
        out = move(out)

    g_mix = dot_tn(mix, dproj).astype(bf16)
    pairs = g_mix[: members * LANES].reshape(members, LANES, width)
    thirds = g_mix[members * LANES :].reshape(members, HEAD_DIM, width)
    g_out = jnp.concatenate([pairs, thirds], axis=1).reshape(width, width)

    draw, sums = attend_back(rand_flat, qkv, res, dctx, heads)

    def strip(a):
        a = a.reshape(a.shape[:-1] + (heads, 4, HEAD_DIM))
        q, k, v = a[..., 0, :] * (HEAD_DIM**-0.5), a[..., 2, :], a[..., 3, :]
        return jnp.stack([q, k, v], axis=-3).reshape(a.shape[:-3] + (3, cols))

    col_sums = strip(sums[0:1])[0]
    pair = jnp.stack([col_sums[0], col_sums[2]]).reshape(2, 1, cols)
    mine = (jnp.arange(members) == group)[None, :, None]
    pair = jnp.where(mine, pair, 0.0).reshape(2, width)
    vec_grads = jnp.concatenate([pair, gvec[0:6]], axis=0).reshape(8, devices, own)
    vec_grads = jnp.transpose(vec_grads, (1, 0, 2)).reshape(devices, 8 * own)
    vec_grads = jnp.concatenate([vec_grads, gbu[0].reshape(devices, -1)], axis=1)
    count = vec_grads.shape[1]

    if direct:
        lines = 8
        padded = jnp.pad(vec_grads, ((0, 0), (0, lines * LANES - count)))
        g_down, g_up, g_out, vec_grads, g_qkv, input_grad = scatter(
            act.reshape(PIECES, -1, act.shape[1]),
            dffn.reshape(PIECES, -1, width),
            hid.reshape(PIECES, -1, width),
            dpre.reshape(PIECES, -1, dpre.shape[1]),
            g_out.reshape(2, 2, 2, -1, width),
            padded.reshape(2, 2, 2, 4 * lines, LANES),
            draw.reshape(members, PIECES, -1, draw.shape[1]),
            x.reshape(members, PIECES, -1, width),
            w_own,
            dres1.reshape(PIECES, -1, width),
            own,
        )
        vec_grads = vec_grads.reshape(-1)[:count]
        input_grad = input_grad.reshape(rows, width).astype(f32)
    else:

        def reduce(a):
            return lax.psum_scatter(a, ALL, scatter_dimension=0, tiled=True).astype(f32)

        g_down, g_up = reduce(dot_tn(act, dffn).astype(bf16)), reduce(dot_tn(hid, dpre).astype(bf16))
        g_out, vec_grads = reduce(g_out), reduce(vec_grads)[0]
        dx = dot_nt(draw, w_own).astype(bf16)
        dx = lax.psum_scatter(dx, GROUP, scatter_dimension=0, tiled=True)
        input_grad = move((dres1 + dx.astype(f32)).astype(bf16)).astype(f32)
        g_qkv = strip(dot_tn(x, draw)).reshape(-1, 2, 2, members // 2, own, 3 * cols)
        g_qkv = jnp.transpose(g_qkv, (0, 2, 1, 3, 4, 5)).reshape(-1, members, own, 3 * cols)
        g_qkv = g_qkv.reshape(-1, 3 * cols).astype(bf16)
        g_qkv = lax.psum_scatter(g_qkv, REST, scatter_dimension=0, tiled=True)
        g_qkv = g_qkv.reshape(members, own, 3 * cols)
        g_qkv = lax.all_to_all(g_qkv, GROUP, split_axis=0, concat_axis=0, tiled=True).astype(f32)
        g_qkv = jnp.transpose(g_qkv.reshape(members, own, 3, cols), (1, 2, 0, 3)).reshape(own, -1)
    v8 = vec_grads[: 8 * own].reshape(8, own)
    return (
        out[None],
        input_grad[None],
        g_qkv,
        v8[0:2],
        g_out,
        v8[2],
        v8[3],
        v8[4],
        g_up,
        vec_grads[8 * own :],
        g_down,
        v8[5],
        v8[6],
        v8[7],
    )


def solution(mesh):
    dp, sp = mesh.shape["dp"], mesh.shape["sp"]
    fine = Mesh(mesh.devices.reshape(dp // 2, 2, 2, sp // 2), ALL)
    dp, sp = ("c", "core"), ("zh", "zl")
    act = P(dp, sp, None)
    mat = P(ALL, None)
    pair = P(None, ALL)
    vec = P(ALL)
    rand = P(dp, sp, None, None)
    return jax.shard_map(
        per_device,
        mesh=fine,
        in_specs=(act, mat, pair, mat, vec, vec, vec, mat, vec, mat, vec, vec, vec, rand, act),
        out_specs=(act, act, mat, pair, mat, vec, vec, vec, mat, vec, mat, vec, vec, vec),
        check_vma=False,
    )
```

profile of v0, /device:TPU:0, one launch (start us, length us, event | category | flops | bytes accessed | tf_op | source)
XLA Modules:
  0.0 391.6 jit_solution(12818780424254584263)
XLA Ops:
  0.7 0.7 copy.51
  1.5 0.6 collective-permute-start
  2.1 1.1 reshape.245
  3.3 0.2 reshape.241
  4.0 0.6 pad_bitcast_fusion.refs_7_
  5.3 0.2 pad_maximum_fusion.1
  5.5 0.4 copy.35
  5.9 0.4 reshape.214
  6.3 0.8 maximum_maximum_fusion.refs_3_
  7.4 0.8 reshape.210.refs_0_.rand_ref
  8.2 139.1 %front.1 = (bf16[4,4,256,768]{3,2,1,0:T(8,128)(2,1)}, bf16[4,256,768]{2,1,0:T(8,128)(2,1)}, bf16[4,256,768]{2,1,0:T(8,128)(2,1)}, bf16[2,2,2,2,48,768]{5,4,3,2,1...) custom-call(s32[558]{0:T(1024)} %reshape.210.refs_0_.rand_ref, ...), custom_call_target="tpu_custom_call" | custom-call | tf_op jit(solution)/shard_map/front/pallas_call | solution.py:994
  147.4 0.9 copy.50
  148.6 0.7 reshape.226.bu_ref
  149.6 0.6 concatenate.23.vec_ref
  150.2 58.1 %chain.1 = (bf16[4,256,768]{2,1,0:T(8,128)(2,1)}, f32[1024,768]{1,0:T(8,128)}, bf16[4,4,384,128]{3,2,1,0:T(8,128)(2,1)}, bf16[1024,768]{1,0:T(8,128)(2,1)}, bf16...) custom-call(bf16[4,4,384,128]{3,2,1,0:T(8,128)(2,1)} %get-tuple-elem, ...), custom_call_target="tpu_custom_call" | custom-call | tf_op jit(solution)/shard_map/chain/pallas_call | solution.py:645
  208.3 3.3 convolution_convert_fusion
  211.6 51.7 %attend_back.1 = (bf16[4096,768]{1,0:T(8,128)(2,1)}, f32[8,768]{1,0:T(8,128)}) custom-call(s32[558]{0:T(1024)} %reshape.210.refs_0_.rand_ref, bf16[64,64,768]{2,1,0:T(8,128)(2,1)} %get-tuple-element.58.qkv_ref, f32[3,4096,128]{2,1,0:T(8,128)} %get-tuple-element.59.res_ref, bf16[4,4,384,128]{3,2,1,0:T(8,128)(2,1)} %get-tuple-element.60.dctx_ref), custom_call_target="tpu_custom_call" | custom-call | tf_op jit(solution)/shard_map/attend_back/pallas_call | solution.py:305
  263.4 0.8 slice_reduce_fusion.1
  264.5 0.9 slice_reduce_fusion
  266.1 0.7 reshape.235.refs_5_
  266.8 1.1 pad_maximum_fusion
  267.8 112.1 %scatter.1 = (f32[96,768]{1,0:T(8,128)}, f32[24,3072]{1,0:T(8,128)}, f32[24,768]{1,0:T(8,128)}, f32[8,128]{1,0:T(8,128)}, f32[24,2304]{1,0:T(8,128)}, /*index=5*/bf16[4,256,768]{2,1,0:T(8,128)(2,1)}) custom-call(bf16[4,256,3072]{2,1,0:T(8,128)(2,1)} %bitcast.74, bf16[4,256,768]{2,1,0:T(8,128)(2,1)} %bitcast.84, bf16[4,256,768]{2,1,0:T(8,128)(2,1)} %bitcast.83, ...), custom_call_target="tpu_custom_call" | custom-call | tf_op jit(solution)/shard_map/scatter/pallas_call | solution.py:1338
  380.0 1.3 slice.131
  381.2 0.7 slice.126
  381.9 1.5 fusion.4
  383.4 0.6 slice.127
  384.1 3.4 bitcast_convert_fusion
  387.5 1.1 copy.60
  388.6 0.7 copy.61
  389.3 0.6 copy.62
  390.0 0.7 copy.63
  390.7 0.7 copy.64
  (79 shorter events, 2.8 us)
Async XLA Ops:
  0.6 3.2 copy-start.7
  0.7 3.2 copy-start.13
  0.7 3.2 copy-start.12
  0.7 3.2 copy-start.11
  0.7 3.2 copy-start.14
  0.7 3.2 copy-start.10
  0.7 3.2 copy-start.9
  0.7 3.2 copy-start.8
  1.5 5.8 %collective-permute-start = (s32[3,62,3]{1,2,0:T(4,128)S(1)}, s32[3,62,3]{1,2,0:T(4,128)S(1)}, u32[]{:S(2)}, u32[]{:S(2)}) collective-permute-start(s32[3,62,3]{1,2,0:T(4,128)S(1)} %bitcast.99), channel_id=1, source_target_pairs={{0,0},{2,4},{4,2},{6,6},{1,1},{3,5},{5,3},{7,7},{8,8},{10,12},{12,... | collective-permute-start | bytes 6704 | tf_op jit(solution)/shard_map/ppermute | solution.py:1378
  211.6 51.8 %copy-start = (bf16[768,768]{1,0:T(8,128)(2,1)}, bf16[768,768]{1,0:T(8,128)(2,1)S(1)}, u32[]{:S(2)}) copy-start(bf16[768,768]{1,0:T(8,128)(2,1)S(1)} %convolution_convert_fusion) | copy-start | bytes 3538948
  211.6 54.0 %copy-start.6 = (f32[8,768]{1,0:T(8,128)S(1)}, f32[8,768]{1,0:T(8,128)}, u32[]{:S(2)}) copy-start(f32[8,768]{1,0:T(8,128)} %get-tuple-element.62) | copy-start | bytes 73732
  263.4 3.4 slice-start
  263.4 3.4 slice-start.1
  384.1 3.4 copy-start.1
  387.5 1.2 copy-start.4
  387.5 1.9 copy-start.5
  387.5 2.5 copy-start.3
  387.5 3.2 copy-start.2
where the time goes:
time: 397 us; the launch traced here: 392 us
  Pallas kernels  361 us (91%)
  local copies, waits for them, and re-layouts  19.3 us (5%)
  other arithmetic  6 us (2%)
    pallas_call x1, Pallas kernels, front(): pl.pallas_call(partial(front_kernel, heads, randoms), out_shape=tuple(out...  139 us
    pallas_call x1, Pallas kernels, scatter(): pl.pallas_call(scatter_kernel, out_shape=tuple(outs), in_specs=[hbm, vmem...  112 us
    pallas_call x1, Pallas kernels, chain(): pl.pallas_call(partial(chain_kernel, groups, direct), grid=(steps,), out_...  58.1 us
    pallas_call x1, Pallas kernels, attend_back(): pl.pallas_call(partial(attend_back_kernel, heads, randoms), out_shape=(ja...  51.7 us
  transfers between devices with their start and end apart: 1, of which 0 were waited for; matrix products, arithmetic and copies ran while one was open for 1% of the time, Pallas kernels for 0%

commit v1 on v0

--- a/solution.py
+++ b/solution.py
@@ -206,7 +206,7 @@
 
     lax.fori_loop(0, length // ROWS, unpack, 0)
 
-    step = 256
+    step = 512
 
     def ends(ref, cols):
         return jnp.concatenate([ref[0:BLOCK, cols], ref[last : last + BLOCK, cols]], axis=0)

time: 397 us -> 394 us (level)
  no operation moved by 1% of the time
where the time goes in v1:
time: 394 us; the launch traced here: 389 us
  Pallas kernels  358 us (91%)
  local copies, waits for them, and re-layouts  19.3 us (5%)
  other arithmetic  6 us (2%)
    pallas_call x1, Pallas kernels, front(): pl.pallas_call(partial(front_kernel, heads, randoms), out_shape=tuple(out...  139 us
    pallas_call x1, Pallas kernels, scatter(): pl.pallas_call(scatter_kernel, out_shape=tuple(outs), in_specs=[hbm, vmem...  112 us
    pallas_call x1, Pallas kernels, chain(): pl.pallas_call(partial(chain_kernel, groups, direct), grid=(steps,), out_...  58.1 us
    pallas_call x1, Pallas kernels, attend_back(): pl.pallas_call(partial(attend_back_kernel, heads, randoms), out_shape=(ja...  49.1 us
  transfers between devices with their start and end apart: 1, of which 0 were waited for; matrix products, arithmetic and copies ran while one was open for 1% of the time, Pallas kernels for 0%

profile of v1, /device:TPU:0, one launch (start us, length us, event | category | flops | bytes accessed | tf_op | source)
XLA Modules:
  0.0 388.9 jit_solution(12051025372096135166)
XLA Ops:
  0.7 0.7 copy.51
  1.5 0.6 collective-permute-start
  2.1 1.1 reshape.245
  3.3 0.2 reshape.241
  4.0 0.6 pad_bitcast_fusion.refs_7_
  5.3 0.2 pad_maximum_fusion.1
  5.5 0.4 copy.35
  5.9 0.4 reshape.214
  6.3 0.8 maximum_maximum_fusion.refs_3_
  7.4 0.8 reshape.210.refs_0_.rand_ref
  8.2 139.1 %front.1 = (bf16[4,4,256,768]{3,2,1,0:T(8,128)(2,1)}, bf16[4,256,768]{2,1,0:T(8,128)(2,1)}, bf16[4,256,768]{2,1,0:T(8,128)(2,1)}, bf16[2,2,2,2,48,768]{5,4,3,2,1...) custom-call(s32[558]{0:T(1024)} %reshape.210.refs_0_.rand_ref, ...), custom_call_target="tpu_custom_call" | custom-call | tf_op jit(solution)/shard_map/front/pallas_call | solution.py:994
  147.4 0.9 copy.50
  148.6 0.7 reshape.226.bu_ref
  149.6 0.6 concatenate.23.vec_ref
  150.2 58.1 %chain.1 = (bf16[4,256,768]{2,1,0:T(8,128)(2,1)}, f32[1024,768]{1,0:T(8,128)}, bf16[4,4,384,128]{3,2,1,0:T(8,128)(2,1)}, bf16[1024,768]{1,0:T(8,128)(2,1)}, bf16...) custom-call(bf16[4,4,384,128]{3,2,1,0:T(8,128)(2,1)} %get-tuple-elem, ...), custom_call_target="tpu_custom_call" | custom-call | tf_op jit(solution)/shard_map/chain/pallas_call | solution.py:645
  208.3 3.3 convolution_convert_fusion
  211.6 49.1 %attend_back.1 = (bf16[4096,768]{1,0:T(8,128)(2,1)}, f32[8,768]{1,0:T(8,128)}) custom-call(s32[558]{0:T(1024)} %reshape.210.refs_0_.rand_ref, bf16[64,64,768]{2,1,0:T(8,128)(2,1)} %get-tuple-element.58.qkv_ref, f32[3,4096,128]{2,1,0:T(8,128)} %get-tuple-element.59.res_ref, bf16[4,4,384,128]{3,2,1,0:T(8,128)(2,1)} %get-tuple-element.60.dctx_ref), custom_call_target="tpu_custom_call" | custom-call | tf_op jit(solution)/shard_map/attend_back/pallas_call | solution.py:305
  260.7 0.8 slice_reduce_fusion.1
  261.8 0.9 slice_reduce_fusion
  263.4 0.7 reshape.235.refs_5_
  264.1 1.1 pad_maximum_fusion
  265.2 112.1 %scatter.1 = (f32[96,768]{1,0:T(8,128)}, f32[24,3072]{1,0:T(8,128)}, f32[24,768]{1,0:T(8,128)}, f32[8,128]{1,0:T(8,128)}, f32[24,2304]{1,0:T(8,128)}, /*index=5*/bf16[4,256,768]{2,1,0:T(8,128)(2,1)}) custom-call(bf16[4,256,3072]{2,1,0:T(8,128)(2,1)} %bitcast.74, bf16[4,256,768]{2,1,0:T(8,128)(2,1)} %bitcast.84, bf16[4,256,768]{2,1,0:T(8,128)(2,1)} %bitcast.83, ...), custom_call_target="tpu_custom_call" | custom-call | tf_op jit(solution)/shard_map/scatter/pallas_call | solution.py:1338
  377.3 1.3 slice.131
  378.6 0.7 slice.126
  379.2 1.5 fusion.4
  380.7 0.6 slice.127
  381.4 3.4 bitcast_convert_fusion
  384.8 1.1 copy.60
  386.0 0.7 copy.61
  386.7 0.6 copy.62
  387.3 0.7 copy.63
  388.0 0.7 copy.64
  (79 shorter events, 2.8 us)
Async XLA Ops:
  0.6 3.2 copy-start.7
  0.7 3.2 copy-start.13
  0.7 3.2 copy-start.12
  0.7 3.2 copy-start.11
  0.7 3.2 copy-start.14
  0.7 3.2 copy-start.10
  0.7 3.2 copy-start.9
  0.7 3.2 copy-start.8
  1.5 5.8 %collective-permute-start = (s32[3,62,3]{1,2,0:T(4,128)S(1)}, s32[3,62,3]{1,2,0:T(4,128)S(1)}, u32[]{:S(2)}, u32[]{:S(2)}) collective-permute-start(s32[3,62,3]{1,2,0:T(4,128)S(1)} %bitcast.99), channel_id=1, source_target_pairs={{0,0},{2,4},{4,2},{6,6},{1,1},{3,5},{5,3},{7,7},{8,8},{10,12},{12,... | collective-permute-start | bytes 6704 | tf_op jit(solution)/shard_map/ppermute | solution.py:1378
  211.6 49.1 %copy-start = (bf16[768,768]{1,0:T(8,128)(2,1)}, bf16[768,768]{1,0:T(8,128)(2,1)S(1)}, u32[]{:S(2)}) copy-start(bf16[768,768]{1,0:T(8,128)(2,1)S(1)} %convolution_convert_fusion) | copy-start | bytes 3538948
  211.6 51.3 %copy-start.6 = (f32[8,768]{1,0:T(8,128)S(1)}, f32[8,768]{1,0:T(8,128)}, u32[]{:S(2)}) copy-start(f32[8,768]{1,0:T(8,128)} %get-tuple-element.62) | copy-start | bytes 73732
  260.7 3.4 slice-start
  260.7 3.4 slice-start.1
  381.4 3.4 copy-start.1
  384.8 1.2 copy-start.4
  384.8 1.9 copy-start.5
  384.8 2.5 copy-start.3
  384.8 3.2 copy-start.2
